TPU v7x, 32 devices: a whole 2x2x4 slice. The times are simulated.
32 devices in a mesh: groups: 2 (over y), tensor: 8 (over z, x), dp: 2 (over core).
Axes of the slice: x: 2, y: 2, z: 4, core: 2. Of those that a mesh axis runs over, the one named last changes fastest.
Arguments:
- activations: bfloat16 [8192, 64, 512], P('tensor', ('groups', 'dp')), parts along dimension 1, may hold values from -6 to 6
- out_grads: bfloat16 [8192, 64, 512], P('tensor', ('groups', 'dp')), parts along dimension 1, may hold values from -6 to 6
- proj_in: bfloat16 [8192, 64], P('tensor'), may hold values from -0.0625 to 0.0625
- proj_out: bfloat16 [8192, 64], P('tensor'), may hold values from -0.0625 to 0.0625
- padding: int32 [64], P(('groups', 'dp')), parts along dimension 0, may hold values from 0 to 255
- queries: float32 [512, 4096], P(('groups', 'dp')), parts along dimension 0, may hold values from -6 to 6
Outputs:
- scores: float32 [64, 256], P(('groups', 'dp')), parts along dimension 0
There are 2 independent parts, one for each index of `groups`. A program takes and returns all parts, laid end to end along the dimension named above; an argument that names none is the same for every part. Nothing has to cross between parts.
All inputs are finite; a program needn't handle non-finite values.
Results may differ from a plain program's by a relative error of at most 0.0003.
Values may be sent and summed in bfloat16 or wider, within the bound.
A program may use at most 128 MiB of HBM per device.

v0:
```python
import jax
import jax.numpy as jnp
from jax import lax
from jax.sharding import PartitionSpec as P


def build_rows(act_proj, grad_proj, padding, seq_total):
    slots = jnp.arange(act_proj.shape[2], dtype=jnp.int32)
    limit = seq_total - padding
    live = (slots[None, :] < limit[:, None]).astype(jnp.float32)
    count = limit.astype(jnp.float32)
    masked = grad_proj * live[None, :, :]
    summed = jnp.einsum("aes,bes->eab", masked, act_proj, precision=lax.Precision.HIGHEST)
    rank = act_proj.shape[0]
    return (summed / count[:, None, None]).reshape(act_proj.shape[1], rank * rank)


def score_all(grad_rows, queries):
    return jnp.dot(
        grad_rows,
        lax.all_gather(queries, "dp", axis=0, tiled=True).T,
        precision=lax.Precision.HIGHEST,
        preferred_element_type=jnp.float32,
    )


def per_device(activations, out_grads, proj_in, proj_out, padding, queries):
    seq_total = activations.shape[2]
    act_part = jnp.einsum("dr,des->res", proj_in, activations, preferred_element_type=jnp.float32)
    grad_part = jnp.einsum("dr,des->res", proj_out, out_grads, preferred_element_type=jnp.float32)
    act_proj, grad_proj = lax.psum((act_part, grad_part), "tensor")
    grad_rows = build_rows(act_proj, grad_proj, padding, seq_total)
    return score_all(grad_rows, queries)


def solution(mesh):
    placed = (
        P("tensor", ("groups", "dp"), None),
        P("tensor", ("groups", "dp"), None),
        P("tensor", None),
        P("tensor", None),
        P(("groups", "dp")),
        P(("groups", "dp"), None),
    )
    return jax.shard_map(
        per_device, mesh=mesh, in_specs=placed, out_specs=P(("groups", "dp"), None), check_vma=False
    )
```

profile of v0, /device:TPU:0, one launch (start us, length us, event | category | flops | bytes accessed | tf_op | source)
XLA Modules:
  0.0 226.5 jit_solution(8134310751694773045)
XLA Ops:
  7.4 0.0 copy-start
  7.4 0.0 copy-start.2
  7.4 0.0 all-reduce.3.cloned.1.call-start
  7.4 0.9 copy-done
  8.3 0.0 copy-start.1
  8.3 29.9 %fusion = f32[64,16,512]{2,0,1:T(8,128)} fusion(bf16[1024,16,512]{2,1,0:T(8,128)(2,1)} %param.6, bf16[1024,64]{0,1:T(8,128)(2,1)S(1)} %copy-done), kind=kOutput, calls=%fused_computation | convolution fusion | flops 1073741824 | bytes 19005440 | tf_op jit(solution)/shard_map/dr,des->res/dot_general | solution.py:29
  38.1 0.0 copy-done.2
  38.1 0.0 copy-done.1
  38.1 10.7 %fusion.2 = f32[64,16,512]{2,0,1:T(8,128)} fusion(bf16[1024,16,512]{2,1,0:T(8,128)(2,1)S(1)} %copy-done.1, bf16[1024,64]{0,1:T(8,128)(2,1)S(1)} %copy-done.2), kind=kOutput, calls=%fused_computation.2 | convolution fusion | flops 1073741824 | bytes 19005440 | tf_op jit(solution)/shard_map/dr,des->res/dot_general | solution.py:30
  48.8 0.0 all-reduce.3.cloned.1.call-update
  48.8 0.0 copy-start.3
  48.8 0.0 all-gather.2.cloned.1.call-start
  48.9 0.5 all-gather.2.cloned.1.call-update
  49.4 0.1 copy-done.3
  49.5 0.1 fusion.12
  49.6 158.7 %all-reduce.3.cloned.1.call-done = (f32[64,16,512]{2,0,1:T(8,128)}, f32[64,16,512]{2,0,1:T(8,128)}) async-done(((f32[64,16,512]{2,0,1:T(8,128)}, f32[64,16,512]{2,0,1:T(8,128)}), (f32[64,16,512]{2,0,1:T(8,128)}, f32[64,16,512]{2,0,1:T(8,128)})) %all-reduce.3.cloned.1.call-update) | async-done | bytes 4194320 | tf_op jit(solution)/shard_map/psum | solution.py:31
  208.3 4.3 %fusion.6 = f32[16,64,64]{2,1,0:T(8,128)S(1)} fusion(f32[64,16,512]{2,0,1:T(8,128)} %get-tuple-element.5, f32[64,16,512]{2,0,1:T(8,128)} %get-tuple-element.6, f32[16,512]{1,0:T(8,128)S(1)} %fusion.12, f32[16]{0:T(128)S(1)} %get-tuple-element.7), kind=kOutput, calls=%fused_computation.6 | convolution fusion | flops 403243008 | bytes 4489280 | tf_op jit(solution)/shard_map/aes,bes->eab/dot_general | solution.py:13
  212.7 0.2 reshape.23
  212.8 0.0 all-gather.2.cloned.1.call-done
  212.9 6.2 %fusion.14 = f32[16,256]{1,0:T(8,128)} fusion(f32[16,4096]{1,0:T(8,128)S(1)} %reshape.23, f32[256,4096]{1,0:T(8,128)} %all-gather.2.cloned.1.call-done), kind=kOutput, calls=%fused_computation.14 | convolution fusion | flops 201326592 | bytes 4472832 | tf_op jit(solution)/shard_map/dot_general | solution.py:19
  (1 shorter events, 0.0 us)
Async XLA Ops:
  7.4 0.9 copy-start
  7.4 30.8 %copy-start.2 = (bf16[1024,64]{0,1:T(8,128)(2,1)S(1)}, bf16[1024,64]{0,1:T(8,128)(2,1)}, u32[]{:S(2)}) copy-start(bf16[1024,64]{0,1:T(8,128)(2,1)} %param.9) | copy-start | bytes 393220
  7.4 200.9 %all-reduce.3.cloned.1.call-start = ((), (), s32[]{:S(2)}) async-start(), calls=%async_computation.1 | async-start | bytes 8388608 | tf_op jit(solution)/shard_map/psum | solution.py:31
  8.3 29.9 %copy-start.1 = (bf16[1024,16,512]{2,1,0:T(8,128)(2,1)S(1)}, bf16[1024,16,512]{2,1,0:T(8,128)(2,1)}, u32[]{:S(2)}) copy-start(bf16[1024,16,512]{2,1,0:T(8,128)(2,1)} %param.7) | copy-start | bytes 50331652
  48.8 0.7 copy-start.3
  48.8 164.0 %all-gather.2.cloned.1.call-start = ((), (), s32[]{:S(2)}) async-start(), calls=%async_computation | async-start | bytes 6291456 | tf_op jit(solution)/shard_map/all_gather | solution.py:21
Sparse Core Ops, SparseCore 0:
  49.0 159.3 all-reduce.2
Sparse Core Ops, SparseCore 1:
  50.9 16.2 all-gather.1
where the time goes:
time: 227 us; the launch traced here: 226 us
  waiting for transfers between devices  159 us (70%)
  matrix products  51 us (22%)
  between operations  14.9 us (7%)
    psum x1, waiting for transfers between devices, per_device(): act_proj, grad_proj = lax.psum((act_part, grad_part), 'tensor')  159 us
    dot_general x1, matrix products, per_device(): jnp.einsum('dr,des->res', proj_in, activations, preferred_element_type=jn...  29.9 us
    dot_general x1, matrix products, per_device(): jnp.einsum('dr,des->res', proj_out, out_grads, preferred_element_type=jnp...  10.7 us
    dot_general x1, matrix products, score_all(): jnp.dot(grad_rows, lax.all_gather(queries, 'dp', axis=0, tiled=True).T, p...  6.15 us
  transfers between devices with their start and end apart: 2, of which 1 were waited for; matrix products, arithmetic and copies ran while one was open for 2% of the time, Pallas kernels for 0%

commit v1 on v0

v1 whole, which is shorter than its diff:
```python
import functools

import jax
import jax.numpy as jnp
from jax import lax
from jax.experimental import pallas as pl
from jax.experimental.pallas import tpu as pltpu
from jax.sharding import PartitionSpec as P

MESH = pl.DeviceIdType.MESH
LEVELS = 32767.0


def quantize(values, data_ref, scale_ref, row):
    top = jnp.maximum(jnp.max(jnp.abs(values), axis=0, keepdims=True), 1e-30)
    data_ref[...] = jnp.round(values * (LEVELS / top)).astype(jnp.int32).astype(jnp.int16)
    step = top * (1.0 / LEVELS)
    tiles = values.shape[1] // 128
    for tile in range(tiles):
        scale_ref[pl.ds(row * tiles + tile, 1), :] = step[:, tile * 128 : (tile + 1) * 128]


def restore(data_ref, scale_ref, row):
    tiles = data_ref.shape[1] // 128
    step = jnp.concatenate([scale_ref[pl.ds(row * tiles + tile, 1), :] for tile in range(tiles)], axis=1)
    return data_ref[...].astype(jnp.int32).astype(jnp.float32) * step


def halves(values):
    high = values.astype(jnp.bfloat16)
    return high, (values - high.astype(jnp.float32)).astype(jnp.bfloat16)


def reduce_and_score(
    n, act_ref, grad_ref, padding_ref, queries_ref, out_ref,
    xs, xs_scale, xr, xr_scale, zs, zs_scale, zr, zr_scale, total, all_queries, query_high, query_low, rows, results,
    xd_sem, xf_sem, zd_sem, zf_sem, q_sem, out_send, out_recv,
):
    examples, rank, seq = act_ref.shape
    own = examples // n
    steps = n // 2
    me, core = lax.axis_index("tensor"), lax.axis_index("dp")
    z, x = me // 2, lax.rem(me, 2)
    parts = (act_ref, grad_ref)

    barrier = pltpu.get_barrier_semaphore()
    for shift in range(1, n):
        pl.semaphore_signal(barrier, inc=1, device_id={"tensor": lax.rem(me + shift, n)}, device_id_type=MESH)
    pl.semaphore_signal(barrier, inc=1, device_id={"dp": 1 - core}, device_id_type=MESH)
    pl.semaphore_wait(barrier, n)

    def send(source, target, send_sem, recv_sem, device):
        return pltpu.make_async_remote_copy(
            src_ref=source, dst_ref=target, send_sem=send_sem, recv_sem=recv_sem, device_id=device, device_id_type=MESH
        )

    def x_copies(c):
        device = {"tensor": z * 2 + (1 - x)}
        return (
            send(xs.at[c], xr.at[c], xd_sem.at[0, c], xd_sem.at[1, c], device),
            send(xs_scale.at[c], xr_scale.at[c], xf_sem.at[0, c], xf_sem.at[1, c], device),
        )

    def z_copies(c):
        goal = lax.rem(z + (steps - 1 - c // own), steps)
        device = {"tensor": goal * 2 + x}
        return (
            send(zs.at[c], zr.at[c], zd_sem.at[0, c], zd_sem.at[1, c], device),
            send(zs_scale.at[c], zr_scale.at[c], zf_sem.at[0, c], zf_sem.at[1, c], device),
        )

    def example(c, parity):
        goal = lax.rem(z + (steps - 1 - c // own), steps)
        return (goal * 2 + parity) * own + lax.rem(c, own)

    def first(c, carry):
        e = example(c, 1 - x)
        for k in range(2):
            quantize(parts[k][e], xs.at[c, k], xs_scale.at[c], k)
        for copy in x_copies(c):
            copy.start()
        return carry

    lax.fori_loop(0, steps * own, first, 0)

    local = pltpu.make_async_copy(queries_ref, all_queries.at[core], q_sem.at[2])
    other = send(queries_ref, all_queries.at[core], q_sem.at[0], q_sem.at[1], {"dp": 1 - core})
    local.start()
    other.start()

    def second(c, carry):
        for copy in x_copies(c):
            copy.wait_recv()
        e = example(c, x)
        for k in range(2):
            quantize(parts[k][e] + restore(xr.at[c, k], xr_scale.at[c], k), zs.at[c, k], zs_scale.at[c], k)
        for copy in z_copies(c):
            copy.start()
        return carry

    sent = (steps - 1) * own
    lax.fori_loop(0, sent, second, 0)

    local.wait()
    other.wait()
    count = queries_ref.shape[0]
    for half in range(2):
        high, low = halves(all_queries[half])
        query_high[half * count : (half + 1) * count] = high
        query_low[half * count : (half + 1) * count] = low

    for i in range(own):
        c = sent + i
        for copy in x_copies(c):
            copy.wait_recv()
        e = example(c, x)
        for k in range(2):
            total[i, k] = parts[k][e] + restore(xr.at[c, k], xr_scale.at[c], k)

    def third(c, carry):
        for copy in z_copies(c):
            copy.wait_recv()
        i = lax.rem(c, own)
        for k in range(2):
            total[i, k] = total[i, k] + restore(zr.at[c, k], zr_scale.at[c], k)
        return carry

    lax.fori_loop(0, sent, third, 0)

    slots = lax.broadcasted_iota(jnp.int32, (1, seq), 1)
    rows[...] = jnp.zeros_like(rows)
    for i in range(own):
        limit = seq - padding_ref[0, me * own + i]
        live = slots < limit
        act = jnp.concatenate(halves(total[i, 0]), axis=0)
        grad = jnp.concatenate(halves(jnp.where(live, total[i, 1], 0.0)), axis=0)
        summed = lax.dot_general(grad, act, (((1,), (1,)), ((), ())), preferred_element_type=jnp.float32)
        summed = summed[:rank, :rank] + summed[:rank, rank:] + summed[rank:, :rank]
        summed = summed / jnp.full((1, 1), limit, jnp.int32).astype(jnp.float32)
        for a in range(rank):
            rows[i : i + 1, a * rank : (a + 1) * rank] = summed[a : a + 1, :]
    row_high, row_low = halves(rows[...])
    stacked = jnp.concatenate([row_high.astype(jnp.float32), row_low.astype(jnp.float32)], axis=0).astype(jnp.bfloat16)
    contract = (((1,), (1,)), ((), ()))
    by_high = lax.dot_general(stacked, query_high[...], contract, preferred_element_type=jnp.float32)
    by_low = lax.dot_general(stacked, query_low[...], contract, preferred_element_type=jnp.float32)
    results[me] = by_high[:8] + by_high[8:] + by_low[:8]

    def result_copy(shift):
        return send(
            results.at[me], results.at[me], out_send.at[shift - 1], out_recv.at[shift - 1],
            {"tensor": lax.rem(me + shift, n)},
        )

    for shift in range(1, n):
        result_copy(shift).start()
    for shift in range(1, n):
        source = lax.rem(me + (n - shift), n)
        send(
            results.at[source], results.at[source], out_send.at[shift - 1], out_recv.at[shift - 1],
            {"tensor": lax.rem(me + shift, n)},
        ).wait_recv()
    for t in range(n):
        out_ref[t * own : (t + 1) * own, :] = results[t][:own]
    for shift in range(1, n):
        result_copy(shift).wait_send()

    def sent_x(c, carry):
        for copy in x_copies(c):
            copy.wait_send()
        return carry

    def sent_z(c, carry):
        for copy in z_copies(c):
            copy.wait_send()
        return carry

    lax.fori_loop(0, steps * own, sent_x, 0)
    lax.fori_loop(0, sent, sent_z, 0)


def fused(n, act_part, grad_part, padding, queries):
    examples, rank, seq = act_part.shape
    own = examples // n
    x_chunks, z_chunks = examples // 2, examples // 2 - own
    scale_rows = 2 * seq // 128
    count, width = queries.shape
    vmem = pl.BlockSpec(memory_space=pltpu.VMEM)
    return pl.pallas_call(
        functools.partial(reduce_and_score, n),
        out_shape=jax.ShapeDtypeStruct((examples, 2 * count), jnp.float32),
        in_specs=[vmem, vmem, pl.BlockSpec(memory_space=pltpu.SMEM), pl.BlockSpec(memory_space=pl.ANY)],
        out_specs=vmem,
        scratch_shapes=[
            pltpu.VMEM((x_chunks, 2, rank, seq), jnp.int16),
            pltpu.VMEM((x_chunks, scale_rows, 128), jnp.float32),
            pltpu.VMEM((x_chunks, 2, rank, seq), jnp.int16),
            pltpu.VMEM((x_chunks, scale_rows, 128), jnp.float32),
            pltpu.VMEM((z_chunks, 2, rank, seq), jnp.int16),
            pltpu.VMEM((z_chunks, scale_rows, 128), jnp.float32),
            pltpu.VMEM((z_chunks, 2, rank, seq), jnp.int16),
            pltpu.VMEM((z_chunks, scale_rows, 128), jnp.float32),
            pltpu.VMEM((own, 2, rank, seq), jnp.float32),
            pltpu.VMEM((2, count, width), jnp.float32),
            pltpu.VMEM((2 * count, width), jnp.bfloat16),
            pltpu.VMEM((2 * count, width), jnp.bfloat16),
            pltpu.VMEM((8, width), jnp.float32),
            pltpu.VMEM((n, 8, 2 * count), jnp.float32),
            pltpu.SemaphoreType.DMA((2, x_chunks)),
            pltpu.SemaphoreType.DMA((2, x_chunks)),
            pltpu.SemaphoreType.DMA((2, z_chunks)),
            pltpu.SemaphoreType.DMA((2, z_chunks)),
            pltpu.SemaphoreType.DMA((3,)),
            pltpu.SemaphoreType.DMA((n - 1,)),
            pltpu.SemaphoreType.DMA((n - 1,)),
        ],
        compiler_params=pltpu.CompilerParams(
            collective_id=0, has_side_effects=True, vmem_limit_bytes=40 << 20
        ),
    )(act_part, grad_part, padding.reshape(1, examples), queries)


def plain(act_part, grad_part, padding, queries):
    act_proj, grad_proj = lax.psum((act_part, grad_part), "tensor")
    examples, rank, seq = act_proj.shape
    limit = seq - padding
    live = (jnp.arange(seq, dtype=jnp.int32)[None, :] < limit[:, None]).astype(jnp.float32)
    summed = jnp.einsum("eas,ebs->eab", grad_proj * live[:, None, :], act_proj, precision=lax.Precision.HIGHEST)
    grad_rows = (summed / limit.astype(jnp.float32)[:, None, None]).reshape(examples, rank * rank)
    gathered = lax.all_gather(queries, "dp", axis=0, tiled=True)
    return jnp.dot(grad_rows, gathered.T, precision=lax.Precision.HIGHEST, preferred_element_type=jnp.float32)


def per_device(n, cores, activations, out_grads, proj_in, proj_out, padding, queries):
    act_part = jnp.einsum("dr,des->ers", proj_in, activations, preferred_element_type=jnp.float32)
    grad_part = jnp.einsum("dr,des->ers", proj_out, out_grads, preferred_element_type=jnp.float32)
    examples = activations.shape[1]
    if cores == 2 and n % 2 == 0 and n >= 4 and examples % n == 0 and examples // n <= 8:
        return fused(n, act_part, grad_part, padding, queries)
    return plain(act_part, grad_part, padding, queries)


def solution(mesh):
    placed = (
        P("tensor", ("groups", "dp"), None),
        P("tensor", ("groups", "dp"), None),
        P("tensor", None),
        P("tensor", None),
        P(("groups", "dp")),
        P(("groups", "dp"), None),
    )
    return jax.shard_map(
        functools.partial(per_device, mesh.shape["tensor"], mesh.shape["dp"]),
        mesh=mesh, in_specs=placed, out_specs=P(("groups", "dp"), None), check_vma=False,
    )
```

time: 227 us -> 70.7 us (0.31)
  waiting for transfers between devices: 159 us -> 0 us
  Pallas kernels: 0 us -> 42.9 us
  matrix products: 51 us -> 26.2 us
  between operations: 14.9 us -> 0.05 us
    psum x1 -> x0, waiting for transfers between devices: 159 us -> none  [per_device(): act_proj, grad_proj = lax.psum((act_part, grad_part), 'tensor')]
    pallas_call x0 -> x1, Pallas kernels: none -> 42.9 us  [fused(): pl.pallas_call(functools.partial(reduce_and_score, n), out_shape=jax.Shap...]
    dot_general x4 -> x2, matrix products: 51 us -> 26.2 us  [the longest x1 13.1 us: per_device(): jnp.einsum('dr,des->ers', proj_in, activations, preferred_element_type=jn...]
  transfers between devices with their start and end apart: 2 -> 0, of which waited for: 1 -> 0; matrix products, arithmetic and copies ran while one was open for 2% -> 0% of each run, Pallas kernels for 0% -> 0%
where the time goes in v1:
time: 70.7 us; the launch traced here: 70.6 us
  Pallas kernels  42.9 us (61%)
  matrix products  26.2 us (37%)
  local copies, waits for them, and re-layouts  1.52 us (2%)
    pallas_call x1, Pallas kernels, fused(): pl.pallas_call(functools.partial(reduce_and_score, n), out_shape=jax.Shap...  42.9 us
    dot_general x1, matrix products, per_device(): jnp.einsum('dr,des->ers', proj_in, activations, preferred_element_type=jn...  13.1 us
    dot_general x1, matrix products, per_device(): jnp.einsum('dr,des->ers', proj_out, out_grads, preferred_element_type=jnp...  13 us
    unnamed x9, local copies, waits for them, and re-layouts  1.52 us

profile of v1, /device:TPU:0, one launch (start us, length us, event | category | flops | bytes accessed | tf_op | source)
XLA Modules:
  0.0 70.6 jit_solution(8822163463299149807)
XLA Ops:
  0.0 0.0 copy-start
  0.0 0.0 copy-start.3
  0.0 0.9 %copy-done = bf16[1024,64]{0,1:T(8,128)(2,1)S(1)} copy-done((bf16[1024,64]{0,1:T(8,128)(2,1)S(1)}, bf16[1024,64]{0,1:T(8,128)(2,1)}, u32[]{:S(2)}) %copy-start) | copy-done | bytes 131096
  0.9 0.0 copy-start.1
  0.9 0.0 copy-start.2
  0.9 13.1 %fusion.4.act_ref = f32[16,64,512]{2,1,0:T(8,128)S(1)} fusion(bf16[1024,16,512]{2,1,0:T(8,128)(2,1)} %param.6, bf16[1024,64]{0,1:T(8,128)(2,1)S(1)} %copy-done), kind=kOutput, calls=%fused_computation.4 | convolution fusion | flops 1073741824 | bytes 19005440 | tf_op jit(solution)/shard_map/dr,des->ers/dot_general | solution.py:235
  14.1 0.0 copy-done.3
  14.1 13.0 %fusion.7.grad_ref = f32[16,64,512]{2,1,0:T(8,128)S(1)} fusion(bf16[1024,16,512]{2,1,0:T(8,128)(2,1)} %param.7, bf16[1024,64]{0,1:T(8,128)(2,1)S(1)} %copy-done.3), kind=kOutput, calls=%fused_computation.5 | convolution fusion | flops 1073741824 | bytes 19005440 | tf_op jit(solution)/shard_map/dr,des->ers/dot_general | solution.py:236
  27.1 0.0 copy-done.1
  27.1 0.0 copy-done.2
  27.1 42.9 %shard_map.64 = f32[16,256]{1,0:T(8,128)S(1)} custom-call(f32[16,64,512]{2,1,0:T(8,128)S(1)} %fusion.4.act_ref, f32[16,64,512]{2,1,0:T(8,128)S(1)} %fusion.7.grad_ref, s32[1,16]{1,0:T(1,128)S(1)} %bitcast.11, f32[128,4096]{1,0:T(8,128)S(1)} %copy-done.1), custom_call_target="tpu_custom_call" | custom-call | tf_op jit(solution)/shard_map/pallas_call | solution.py:189
  70.0 0.6 copy.18
Async XLA Ops:
  0.0 0.9 %copy-start = (bf16[1024,64]{0,1:T(8,128)(2,1)S(1)}, bf16[1024,64]{0,1:T(8,128)(2,1)}, u32[]{:S(2)}) copy-start(bf16[1024,64]{0,1:T(8,128)(2,1)} %param.8) | copy-start | bytes 393220
  0.0 14.1 %copy-start.3 = (bf16[1024,64]{0,1:T(8,128)(2,1)S(1)}, bf16[1024,64]{0,1:T(8,128)(2,1)}, u32[]{:S(2)}) copy-start(bf16[1024,64]{0,1:T(8,128)(2,1)} %param.9) | copy-start | bytes 393220
  0.9 26.2 %copy-start.1 = (f32[128,4096]{1,0:T(8,128)S(1)}, f32[128,4096]{1,0:T(8,128)}, u32[]{:S(2)}) copy-start(f32[128,4096]{1,0:T(8,128)} %queries_ref.1) | copy-start | bytes 6291460
  0.9 26.2 %copy-start.2 = (s32[16]{0:T(128)S(1)}, s32[16]{0:T(128)}, u32[]{:S(2)}) copy-start(s32[16]{0:T(128)} %param.10) | copy-start | bytes 196

commit v2 on v1

v2 whole, which is shorter than its diff:
```python
import functools

import jax
import jax.numpy as jnp
from jax import lax
from jax.experimental import pallas as pl
from jax.experimental.pallas import tpu as pltpu
from jax.sharding import PartitionSpec as P

MESH = pl.DeviceIdType.MESH
LEVELS = 32767.0


LANES = 128


def quantize(values, data_ref, scale_ref, row):
    top = jnp.maximum(jnp.max(jnp.abs(values), axis=0, keepdims=True), 1e-30)
    data_ref[...] = jnp.round(values * (LEVELS / top)).astype(jnp.int32).astype(jnp.int16)
    scale_ref[row : row + 1, :] = top * (1.0 / LEVELS)


def restore(data_ref, scale_ref, row):
    return data_ref[...].astype(jnp.int32).astype(jnp.float32) * scale_ref[row : row + 1, :]


def halves(values):
    high = values.astype(jnp.bfloat16)
    return high, (values - high.astype(jnp.float32)).astype(jnp.bfloat16)


def example_major(block, turned):
    for d in range(0, block.shape[0], 16):
        rows = jnp.swapaxes(block[d : d + 16], 0, 1)
        for e in range(16):
            turned[e // 2, d : d + 16, (e % 2) * LANES : (e % 2 + 1) * LANES] = rows[e]


def project(weights, turned, part):
    for pair in range(turned.shape[0]):
        both = lax.dot_general(
            weights[...], turned[pair], (((1,), (0,)), ((), ())), preferred_element_type=jnp.float32
        )
        part[2 * pair] = both[:, :LANES]
        part[2 * pair + 1] = both[:, LANES:]


def attribute(
    n, act_ref, grad_ref, proj_in_ref, proj_out_ref, padding_ref, queries_ref, out_ref,
    act_block, grad_block, act_turned, grad_turned, weights, part,
    xs, xs_scale, xr, xr_scale, zs, zs_scale, zr, zr_scale, total, all_queries, query_high, query_low, rows, results,
    in_sem, xd_sem, xf_sem, zd_sem, zf_sem, q_sem, out_send, out_recv,
):
    examples, seq = act_ref.shape[1:]
    rank = proj_in_ref.shape[1]
    own = examples // n
    steps = n // 2
    tiles = seq // LANES
    me, core = lax.axis_index("tensor"), lax.axis_index("dp")
    z, x = me // 2, lax.rem(me, 2)

    def fetch(source, block, tile, sem):
        lanes = pl.ds(pl.multiple_of(tile * LANES, LANES), LANES)
        return pltpu.make_async_copy(source.at[:, :, lanes], block, in_sem.at[sem])

    fetch(act_ref, act_block, 0, 0).start()
    fetch(grad_ref, grad_block, 0, 1).start()

    barrier = pltpu.get_barrier_semaphore()
    for shift in range(1, n):
        pl.semaphore_signal(barrier, inc=1, device_id={"tensor": lax.rem(me + shift, n)}, device_id_type=MESH)
    pl.semaphore_signal(barrier, inc=1, device_id={"dp": 1 - core}, device_id_type=MESH)

    weights[0] = proj_in_ref[...].astype(jnp.float32).T.astype(jnp.bfloat16)
    weights[1] = proj_out_ref[...].astype(jnp.float32).T.astype(jnp.bfloat16)

    def send(source, target, send_sem, recv_sem, device):
        return pltpu.make_async_remote_copy(
            src_ref=source, dst_ref=target, send_sem=send_sem, recv_sem=recv_sem, device_id=device, device_id_type=MESH
        )

    def owner(j):
        return lax.rem(z + (steps - 1 - j), steps)

    def x_copies(tile, j):
        device = {"tensor": z * 2 + (1 - x)}
        return (
            send(xs.at[tile, j], xr.at[tile, j], xd_sem.at[0, tile, j], xd_sem.at[1, tile, j], device),
            send(xs_scale.at[tile, j], xr_scale.at[tile, j], xf_sem.at[0, tile, j], xf_sem.at[1, tile, j], device),
        )

    def z_copies(tile, j):
        device = {"tensor": owner(j) * 2 + x}
        return (
            send(zs.at[tile, j], zr.at[tile, j], zd_sem.at[0, tile, j], zd_sem.at[1, tile, j], device),
            send(zs_scale.at[tile, j], zr_scale.at[tile, j], zf_sem.at[0, tile, j], zf_sem.at[1, tile, j], device),
        )

    pairs = [(i, k) for i in range(own) for k in range(2)]

    def to_x(tile):
        def one(j, carry):
            base = (owner(j) * 2 + (1 - x)) * own
            for i, k in pairs:
                quantize(part[tile, k, base + i], xs.at[tile, j, i, k], xs_scale.at[tile, j], 2 * i + k)
            for copy in x_copies(tile, j):
                copy.start()
            return carry

        lax.fori_loop(0, steps, one, 0)

    def x_to_z(tile):
        def one(j, carry):
            for copy in x_copies(tile, j):
                copy.wait_recv()
            base = (owner(j) * 2 + x) * own
            for i, k in pairs:
                arrived = restore(xr.at[tile, j, i, k], xr_scale.at[tile, j], 2 * i + k)
                quantize(part[tile, k, base + i] + arrived, zs.at[tile, j, i, k], zs_scale.at[tile, j], 2 * i + k)
            for copy in z_copies(tile, j):
                copy.start()
            return carry

        lax.fori_loop(0, steps - 1, one, 0)

    def local_queries():
        return pltpu.make_async_copy(queries_ref, all_queries.at[core], q_sem.at[2])

    def other_queries():
        return send(queries_ref, all_queries.at[core], q_sem.at[0], q_sem.at[1], {"dp": 1 - core})

    def project_tile(tile, carry):
        fetch(act_ref, act_block, tile, 0).wait()
        example_major(act_block, act_turned)

        @pl.when(tile < tiles - 1)
        def _():
            fetch(act_ref, act_block, tile + 1, 0).start()

        fetch(grad_ref, grad_block, tile, 1).wait()
        example_major(grad_block, grad_turned)
        project(weights.at[0], act_turned, part.at[tile, 0])

        @pl.when(tile < tiles - 1)
        def _():
            fetch(grad_ref, grad_block, tile + 1, 1).start()

        project(weights.at[1], grad_turned, part.at[tile, 1])

        @pl.when(tile == 0)
        def _():
            pl.semaphore_wait(barrier, n)

        to_x(tile)

        @pl.when(tile == 0)
        def _():
            local_queries().start()
            other_queries().start()

        @pl.when(tile > 0)
        def _():
            x_to_z(tile - 1)

        return carry

    lax.fori_loop(0, tiles, project_tile, 0)

    local_queries().wait()
    other_queries().wait()
    count = queries_ref.shape[0]
    for half in range(2):
        high, low = halves(all_queries[half])
        query_high[half * count : (half + 1) * count] = high
        query_low[half * count : (half + 1) * count] = low

    x_to_z(tiles - 1)

    def finish(tile, carry):
        for copy in x_copies(tile, steps - 1):
            copy.wait_recv()
        base = (z * 2 + x) * own
        sums = [
            part[tile, k, base + i] + restore(xr.at[tile, steps - 1, i, k], xr_scale.at[tile, steps - 1], 2 * i + k)
            for i, k in pairs
        ]
        for j in range(steps - 1):
            for copy in z_copies(tile, j):
                copy.wait_recv()
            sums = [
                s + restore(zr.at[tile, j, i, k], zr_scale.at[tile, j], 2 * i + k) for s, (i, k) in zip(sums, pairs)
            ]
        for s, (i, k) in zip(sums, pairs):
            total[tile, i, k] = s
        return carry

    lax.fori_loop(0, tiles, finish, 0)

    slots = lax.broadcasted_iota(jnp.int32, (1, seq), 1)
    rows[...] = jnp.zeros_like(rows)
    contract = (((1,), (1,)), ((), ()))
    for i in range(own):
        limit = seq - padding_ref[0, me * own + i]
        act = jnp.concatenate([total[tile, i, 0] for tile in range(tiles)], axis=1)
        grad = jnp.concatenate([total[tile, i, 1] for tile in range(tiles)], axis=1)
        act = jnp.concatenate(halves(act), axis=0)
        grad = jnp.concatenate(halves(jnp.where(slots < limit, grad, 0.0)), axis=0)
        summed = lax.dot_general(grad, act, contract, preferred_element_type=jnp.float32)
        summed = summed[:rank, :rank] + summed[:rank, rank:] + summed[rank:, :rank]
        summed = summed / jnp.full((1, 1), limit, jnp.int32).astype(jnp.float32)
        for a in range(rank):
            rows[i : i + 1, a * rank : (a + 1) * rank] = summed[a : a + 1, :]
    row_high, row_low = halves(rows[...])
    stacked = jnp.concatenate([row_high.astype(jnp.float32), row_low.astype(jnp.float32)], axis=0).astype(jnp.bfloat16)
    by_high = lax.dot_general(stacked, query_high[...], contract, preferred_element_type=jnp.float32)
    by_low = lax.dot_general(stacked, query_low[...], contract, preferred_element_type=jnp.float32)
    results[me] = by_high[:8] + by_high[8:] + by_low[:8]

    def result_copy(shift, slot):
        return send(
            results.at[slot], results.at[slot], out_send.at[shift - 1], out_recv.at[shift - 1],
            {"tensor": lax.rem(me + shift, n)},
        )

    for shift in range(1, n):
        result_copy(shift, me).start()

    def sent(tile, carry):
        for j in range(steps):
            for copy in x_copies(tile, j):
                copy.wait_send()
        for j in range(steps - 1):
            for copy in z_copies(tile, j):
                copy.wait_send()
        return carry

    lax.fori_loop(0, tiles, sent, 0)
    for shift in range(1, n):
        result_copy(shift, lax.rem(me + (n - shift), n)).wait_recv()
    for t in range(n):
        out_ref[t * own : (t + 1) * own, :] = results[t][:own]
    for shift in range(1, n):
        result_copy(shift, me).wait_send()


def fused(n, activations, out_grads, proj_in, proj_out, padding, queries):
    features, examples, seq = activations.shape
    rank = proj_in.shape[1]
    own, steps, tiles = examples // n, n // 2, seq // LANES
    count, width = queries.shape
    vmem, hbm = pl.BlockSpec(memory_space=pltpu.VMEM), pl.BlockSpec(memory_space=pl.ANY)

    def crossing(chunks):
        return [
            pltpu.VMEM((tiles, chunks, own, 2, rank, LANES), jnp.int16),
            pltpu.VMEM((tiles, chunks, 8, LANES), jnp.float32),
        ] * 2

    return pl.pallas_call(
        functools.partial(attribute, n),
        out_shape=jax.ShapeDtypeStruct((examples, 2 * count), jnp.float32),
        in_specs=[hbm, hbm, vmem, vmem, pl.BlockSpec(memory_space=pltpu.SMEM), hbm],
        out_specs=vmem,
        scratch_shapes=[
            pltpu.VMEM((features, examples, LANES), jnp.bfloat16),
            pltpu.VMEM((features, examples, LANES), jnp.bfloat16),
            pltpu.VMEM((examples // 2, features, 2 * LANES), jnp.bfloat16),
            pltpu.VMEM((examples // 2, features, 2 * LANES), jnp.bfloat16),
            pltpu.VMEM((2, rank, features), jnp.bfloat16),
            pltpu.VMEM((tiles, 2, examples, rank, LANES), jnp.float32),
            *crossing(steps),
            *crossing(steps - 1),
            pltpu.VMEM((tiles, own, 2, rank, LANES), jnp.float32),
            pltpu.VMEM((2, count, width), jnp.float32),
            pltpu.VMEM((2 * count, width), jnp.bfloat16),
            pltpu.VMEM((2 * count, width), jnp.bfloat16),
            pltpu.VMEM((8, width), jnp.float32),
            pltpu.VMEM((n, 8, 2 * count), jnp.float32),
            pltpu.SemaphoreType.DMA((2,)),
            pltpu.SemaphoreType.DMA((2, tiles, steps)),
            pltpu.SemaphoreType.DMA((2, tiles, steps)),
            pltpu.SemaphoreType.DMA((2, tiles, steps - 1)),
            pltpu.SemaphoreType.DMA((2, tiles, steps - 1)),
            pltpu.SemaphoreType.DMA((3,)),
            pltpu.SemaphoreType.DMA((n - 1,)),
            pltpu.SemaphoreType.DMA((n - 1,)),
        ],
        compiler_params=pltpu.CompilerParams(
            collective_id=0, has_side_effects=True, vmem_limit_bytes=48 << 20
        ),
    )(activations, out_grads, proj_in, proj_out, padding.reshape(1, examples), queries)


def plain(act_part, grad_part, padding, queries):
    act_proj, grad_proj = lax.psum((act_part, grad_part), "tensor")
    examples, rank, seq = act_proj.shape
    limit = seq - padding
    live = (jnp.arange(seq, dtype=jnp.int32)[None, :] < limit[:, None]).astype(jnp.float32)
    summed = jnp.einsum("eas,ebs->eab", grad_proj * live[:, None, :], act_proj, precision=lax.Precision.HIGHEST)
    grad_rows = (summed / limit.astype(jnp.float32)[:, None, None]).reshape(examples, rank * rank)
    gathered = lax.all_gather(queries, "dp", axis=0, tiled=True)
    return jnp.dot(grad_rows, gathered.T, precision=lax.Precision.HIGHEST, preferred_element_type=jnp.float32)


def per_device(n, cores, activations, out_grads, proj_in, proj_out, padding, queries):
    features, examples, seq = activations.shape
    whole_tiles = examples == 16 and features % 16 == 0 and seq % LANES == 0
    if cores == 2 and n % 2 == 0 and n >= 4 and examples % n == 0 and examples // n <= 4 and whole_tiles:
        return fused(n, activations, out_grads, proj_in, proj_out, padding, queries)
    act_part = jnp.einsum("dr,des->ers", proj_in, activations, preferred_element_type=jnp.float32)
    grad_part = jnp.einsum("dr,des->ers", proj_out, out_grads, preferred_element_type=jnp.float32)
    return plain(act_part, grad_part, padding, queries)


def solution(mesh):
    placed = (
        P("tensor", ("groups", "dp"), None),
        P("tensor", ("groups", "dp"), None),
        P("tensor", None),
        P("tensor", None),
        P(("groups", "dp")),
        P(("groups", "dp"), None),
    )
    return jax.shard_map(
        functools.partial(per_device, mesh.shape["tensor"], mesh.shape["dp"]),
        mesh=mesh, in_specs=placed, out_specs=P(("groups", "dp"), None), check_vma=False,
    )
```

time: 70.7 us -> 50.9 us (0.72)
  matrix products: 26.2 us -> 0 us
  local copies, waits for them, and re-layouts: 1.52 us -> 5 us
  Pallas kernels: 42.9 us -> 45.6 us
    dot_general x2 -> x0, matrix products: 26.2 us -> none  [the longest x1 13.1 us: per_device(): jnp.einsum('dr,des->ers', proj_in, activations, preferred_element_type=jn...]
    unnamed x9 -> x7, local copies, waits for them, and re-layouts: 1.52 us -> 5 us
    pallas_call x1, Pallas kernels: 42.9 us -> 45.6 us  [fused(): pl.pallas_call(functools.partial(attribute, n), out_shape=jax.ShapeDtypeS...]
where the time goes in v2:
time: 50.9 us; the launch traced here: 50.7 us
  Pallas kernels  45.6 us (90%)
  local copies, waits for them, and re-layouts  5 us (10%)
    pallas_call x1, Pallas kernels, fused(): pl.pallas_call(functools.partial(attribute, n), out_shape=jax.ShapeDtypeS...  45.6 us
    unnamed x7, local copies, waits for them, and re-layouts  5 us

profile of v2, /device:TPU:0, one launch (start us, length us, event | category | flops | bytes accessed | tf_op | source)
XLA Modules:
  0.0 50.7 jit_solution(10179107447684127905)
XLA Ops:
  0.0 1.1 %copy.7.proj_in_ref = bf16[1024,64]{1,0:T(8,128)(2,1)S(1)} copy(bf16[1024,64]{0,1:T(8,128)(2,1)} %param.8) | data formatting | bytes 262144 | tf_op args[2]
  1.1 1.1 %copy.8.proj_out_ref = bf16[1024,64]{1,0:T(8,128)(2,1)S(1)} copy(bf16[1024,64]{0,1:T(8,128)(2,1)} %param.9) | data formatting | bytes 262144 | tf_op args[3]
  2.2 0.0 copy-start
  2.2 1.6 %copy-done = f32[128,4096]{1,0:T(8,128)S(1)} copy-done((f32[128,4096]{1,0:T(8,128)S(1)}, f32[128,4096]{1,0:T(8,128)}, u32[]{:S(2)}) %copy-start) | copy-done | bytes 2097176
  3.8 0.0 copy-start.1
  3.8 0.7 %copy-done.1 = s32[16]{0:T(128)S(1)} copy-done((s32[16]{0:T(128)S(1)}, s32[16]{0:T(128)}, u32[]{:S(2)}) %copy-start.1) | copy-done | bytes 88
  4.4 45.6 %shard_map.64 = f32[16,256]{1,0:T(8,128)S(1)} custom-call(bf16[1024,16,512]{2,1,0:T(8,128)(2,1)} %act_ref.1, bf16[1024,16,512]{2,1,0:T(8,128)(2,1)} %grad_ref.1, bf16[1024,64]{1,0:T(8,128)(2,1)S(1)} %copy.7.proj_in_ref, bf16[1024,64]{1,0:T(8,128)(2,1)S(1)} %copy.8.proj_out_ref, s32[1,16]{1,0:T(1,128)S(1)} %bitcast.1, f32[128,4096]{1,0:T(8,128)S(1)} %copy-done), custom_call_target="tpu_custom_call" | custom-call | tf_op jit(solution)/shard_map/pallas_call | solution.py:259
  50.1 0.6 %copy.10 = f32[16,256]{1,0:T(8,128)} copy(f32[16,256]{1,0:T(8,128)S(1)} %shard_map.64) | data formatting | bytes 32768
Async XLA Ops:
  2.2 1.6 %copy-start = (f32[128,4096]{1,0:T(8,128)S(1)}, f32[128,4096]{1,0:T(8,128)}, u32[]{:S(2)}) copy-start(f32[128,4096]{1,0:T(8,128)} %queries_ref.1) | copy-start | bytes 6291460
  3.8 0.7 %copy-start.1 = (s32[16]{0:T(128)S(1)}, s32[16]{0:T(128)}, u32[]{:S(2)}) copy-start(s32[16]{0:T(128)} %param.10) | copy-start | bytes 196

commit v3 on v2

--- a/solution.py
+++ b/solution.py
@@ -1,4 +1,5 @@
 import functools
+import math
 
 import jax
 import jax.numpy as jnp
@@ -52,7 +53,7 @@
     in_sem, xd_sem, xf_sem, zd_sem, zf_sem, q_sem, out_send, out_recv,
 ):
     examples, seq = act_ref.shape[1:]
-    rank = proj_in_ref.shape[1]
+    rank = proj_in_ref.shape[0]
     own = examples // n
     steps = n // 2
     tiles = seq // LANES
@@ -65,14 +66,19 @@
 
     fetch(act_ref, act_block, 0, 0).start()
     fetch(grad_ref, grad_block, 0, 1).start()
+    factors = [
+        pltpu.make_async_copy(ref, weights.at[k], in_sem.at[2 + k]) for k, ref in enumerate((proj_in_ref, proj_out_ref))
+    ]
+    for copy in factors:
+        copy.start()
 
     barrier = pltpu.get_barrier_semaphore()
     for shift in range(1, n):
         pl.semaphore_signal(barrier, inc=1, device_id={"tensor": lax.rem(me + shift, n)}, device_id_type=MESH)
     pl.semaphore_signal(barrier, inc=1, device_id={"dp": 1 - core}, device_id_type=MESH)
 
-    weights[0] = proj_in_ref[...].astype(jnp.float32).T.astype(jnp.bfloat16)
-    weights[1] = proj_out_ref[...].astype(jnp.float32).T.astype(jnp.bfloat16)
+    for copy in factors:
+        copy.wait()
 
     def send(source, target, send_sem, recv_sem, device):
         return pltpu.make_async_remote_copy(
@@ -82,11 +88,11 @@
     def owner(j):
         return lax.rem(z + (steps - 1 - j), steps)
 
-    def x_copies(tile, j):
-        device = {"tensor": z * 2 + (1 - x)}
+    def x_copies(tile, k, j):
+        device, at = {"tensor": z * 2 + (1 - x)}, (tile, k, j)
         return (
-            send(xs.at[tile, j], xr.at[tile, j], xd_sem.at[0, tile, j], xd_sem.at[1, tile, j], device),
-            send(xs_scale.at[tile, j], xr_scale.at[tile, j], xf_sem.at[0, tile, j], xf_sem.at[1, tile, j], device),
+            send(xs.at[at], xr.at[at], xd_sem.at[0, *at], xd_sem.at[1, *at], device),
+            send(xs_scale.at[at], xr_scale.at[at], xf_sem.at[0, *at], xf_sem.at[1, *at], device),
         )
 
     def z_copies(tile, j):
@@ -98,12 +104,12 @@
 
     pairs = [(i, k) for i in range(own) for k in range(2)]
 
-    def to_x(tile):
+    def to_x(tile, k):
         def one(j, carry):
             base = (owner(j) * 2 + (1 - x)) * own
-            for i, k in pairs:
-                quantize(part[tile, k, base + i], xs.at[tile, j, i, k], xs_scale.at[tile, j], 2 * i + k)
-            for copy in x_copies(tile, j):
+            for i in range(own):
+                quantize(part[tile, k, base + i], xs.at[tile, k, j, i], xs_scale.at[tile, k, j], i)
+            for copy in x_copies(tile, k, j):
                 copy.start()
             return carry
 
@@ -111,11 +117,11 @@
 
     def x_to_z(tile):
         def one(j, carry):
-            for copy in x_copies(tile, j):
+            for copy in (*x_copies(tile, 0, j), *x_copies(tile, 1, j)):
                 copy.wait_recv()
             base = (owner(j) * 2 + x) * own
             for i, k in pairs:
-                arrived = restore(xr.at[tile, j, i, k], xr_scale.at[tile, j], 2 * i + k)
+                arrived = restore(xr.at[tile, k, j, i], xr_scale.at[tile, k, j], i)
                 quantize(part[tile, k, base + i] + arrived, zs.at[tile, j, i, k], zs_scale.at[tile, j], 2 * i + k)
             for copy in z_copies(tile, j):
                 copy.start()
@@ -137,9 +143,12 @@
         def _():
             fetch(act_ref, act_block, tile + 1, 0).start()
 
+        project(weights.at[0], act_turned, part.at[tile, 0])
+
+        to_x(tile, 0)
+
         fetch(grad_ref, grad_block, tile, 1).wait()
         example_major(grad_block, grad_turned)
-        project(weights.at[0], act_turned, part.at[tile, 0])
 
         @pl.when(tile < tiles - 1)
         def _():
@@ -147,16 +156,7 @@
 
         project(weights.at[1], grad_turned, part.at[tile, 1])
 
-        @pl.when(tile == 0)
-        def _():
-            pl.semaphore_wait(barrier, n)
-
-        to_x(tile)
-
-        @pl.when(tile == 0)
-        def _():
-            local_queries().start()
-            other_queries().start()
+        to_x(tile, 1)
 
         @pl.when(tile > 0)
         def _():
@@ -164,6 +164,9 @@
 
         return carry
 
+    pl.semaphore_wait(barrier, n)
+    other_queries().start()
+    local_queries().start()
     lax.fori_loop(0, tiles, project_tile, 0)
 
     local_queries().wait()
@@ -177,11 +180,11 @@
     x_to_z(tiles - 1)
 
     def finish(tile, carry):
-        for copy in x_copies(tile, steps - 1):
+        for copy in (*x_copies(tile, 0, steps - 1), *x_copies(tile, 1, steps - 1)):
             copy.wait_recv()
         base = (z * 2 + x) * own
         sums = [
-            part[tile, k, base + i] + restore(xr.at[tile, steps - 1, i, k], xr_scale.at[tile, steps - 1], 2 * i + k)
+            part[tile, k, base + i] + restore(xr.at[tile, k, steps - 1, i], xr_scale.at[tile, k, steps - 1], i)
             for i, k in pairs
         ]
         for j in range(steps - 1):
@@ -227,7 +230,7 @@
 
     def sent(tile, carry):
         for j in range(steps):
-            for copy in x_copies(tile, j):
+            for copy in (*x_copies(tile, 0, j), *x_copies(tile, 1, j)):
                 copy.wait_send()
         for j in range(steps - 1):
             for copy in z_copies(tile, j):
@@ -250,16 +253,16 @@
     count, width = queries.shape
     vmem, hbm = pl.BlockSpec(memory_space=pltpu.VMEM), pl.BlockSpec(memory_space=pl.ANY)
 
-    def crossing(chunks):
+    def crossing(lead, blocks):
         return [
-            pltpu.VMEM((tiles, chunks, own, 2, rank, LANES), jnp.int16),
-            pltpu.VMEM((tiles, chunks, 8, LANES), jnp.float32),
+            pltpu.VMEM((*lead, *blocks, rank, LANES), jnp.int16),
+            pltpu.VMEM((*lead, math.prod(blocks), LANES), jnp.float32),
         ] * 2
 
     return pl.pallas_call(
         functools.partial(attribute, n),
         out_shape=jax.ShapeDtypeStruct((examples, 2 * count), jnp.float32),
-        in_specs=[hbm, hbm, vmem, vmem, pl.BlockSpec(memory_space=pltpu.SMEM), hbm],
+        in_specs=[hbm, hbm, hbm, hbm, pl.BlockSpec(memory_space=pltpu.SMEM), hbm],
         out_specs=vmem,
         scratch_shapes=[
             pltpu.VMEM((features, examples, LANES), jnp.bfloat16),
@@ -268,17 +271,17 @@
             pltpu.VMEM((examples // 2, features, 2 * LANES), jnp.bfloat16),
             pltpu.VMEM((2, rank, features), jnp.bfloat16),
             pltpu.VMEM((tiles, 2, examples, rank, LANES), jnp.float32),
-            *crossing(steps),
-            *crossing(steps - 1),
+            *crossing((tiles, 2, steps), (own,)),
+            *crossing((tiles, steps - 1), (own, 2)),
             pltpu.VMEM((tiles, own, 2, rank, LANES), jnp.float32),
             pltpu.VMEM((2, count, width), jnp.float32),
             pltpu.VMEM((2 * count, width), jnp.bfloat16),
             pltpu.VMEM((2 * count, width), jnp.bfloat16),
             pltpu.VMEM((8, width), jnp.float32),
             pltpu.VMEM((n, 8, 2 * count), jnp.float32),
-            pltpu.SemaphoreType.DMA((2,)),
-            pltpu.SemaphoreType.DMA((2, tiles, steps)),
-            pltpu.SemaphoreType.DMA((2, tiles, steps)),
+            pltpu.SemaphoreType.DMA((4,)),
+            pltpu.SemaphoreType.DMA((2, tiles, 2, steps)),
+            pltpu.SemaphoreType.DMA((2, tiles, 2, steps)),
             pltpu.SemaphoreType.DMA((2, tiles, steps - 1)),
             pltpu.SemaphoreType.DMA((2, tiles, steps - 1)),
             pltpu.SemaphoreType.DMA((3,)),
@@ -288,7 +291,7 @@
         compiler_params=pltpu.CompilerParams(
             collective_id=0, has_side_effects=True, vmem_limit_bytes=48 << 20
         ),
-    )(activations, out_grads, proj_in, proj_out, padding.reshape(1, examples), queries)
+    )(activations, out_grads, proj_in.T, proj_out.T, padding.reshape(1, examples), queries)
 
 
 def plain(act_part, grad_part, padding, queries):

time: 50.9 us -> 51.5 us (1.012)
  Pallas kernels: 45.6 us -> 46.6 us
    pallas_call x1, Pallas kernels: 45.6 us -> 46.6 us  [fused(): pl.pallas_call(functools.partial(attribute, n), out_shape=jax.ShapeDtypeS...]
    unnamed x7 -> x9, local copies, waits for them, and re-layouts: 5 us -> 4.66 us
where the time goes in v3:
time: 51.5 us; the launch traced here: 51.3 us
  Pallas kernels  46.6 us (90%)
  local copies, waits for them, and re-layouts  4.66 us (9%)
    pallas_call x1, Pallas kernels, fused(): pl.pallas_call(functools.partial(attribute, n), out_shape=jax.ShapeDtypeS...  46.6 us
    unnamed x9, local copies, waits for them, and re-layouts  4.66 us

profile of v3, /device:TPU:0, one launch (start us, length us, event | category | flops | bytes accessed | tf_op | source)
XLA Modules:
  0.0 51.3 jit_solution(8258165111754617096)
XLA Ops:
  0.0 0.0 copy-start
  0.0 1.6 %copy-done = f32[128,4096]{1,0:T(8,128)S(1)} copy-done((f32[128,4096]{1,0:T(8,128)S(1)}, f32[128,4096]{1,0:T(8,128)}, u32[]{:S(2)}) %copy-start) | copy-done | bytes 2097176
  1.6 0.0 copy-start.1
  1.6 0.9 %copy-done.1 = bf16[1024,64]{0,1:T(8,128)(2,1)S(1)} copy-done((bf16[1024,64]{0,1:T(8,128)(2,1)S(1)}, bf16[1024,64]{0,1:T(8,128)(2,1)}, u32[]{:S(2)}) %copy-start.1) | copy-done | bytes 131096
  2.5 0.0 copy-start.2
  2.5 0.9 %copy-done.2 = bf16[1024,64]{0,1:T(8,128)(2,1)S(1)} copy-done((bf16[1024,64]{0,1:T(8,128)(2,1)S(1)}, bf16[1024,64]{0,1:T(8,128)(2,1)}, u32[]{:S(2)}) %copy-start.2) | copy-done | bytes 131096
  3.4 0.0 copy-start.3
  3.4 0.7 %copy-done.3 = s32[16]{0:T(128)S(1)} copy-done((s32[16]{0:T(128)S(1)}, s32[16]{0:T(128)}, u32[]{:S(2)}) %copy-start.3) | copy-done | bytes 88
  4.1 46.6 %shard_map.64 = f32[16,256]{1,0:T(8,128)S(1)} custom-call(bf16[1024,16,512]{2,1,0:T(8,128)(2,1)} %act_ref.1, bf16[1024,16,512]{2,1,0:T(8,128)(2,1)} %grad_ref.1, bf16[64,1024]{1,0:T(8,128)(2,1)S(1)} %bitcast.3, bf16[64,1024]{1,0:T(8,128)(2,1)S(1)} %bitcast.4, s32[1,16]{1,0:T(1,128)S(1)} %bitcast.5, f32[128,4096]{1,0:T(8,128)S(1)} %copy-done), custom_call_target="tpu_custom_call" | custom-call | tf_op jit(solution)/shard_map/pallas_call | solution.py:262
  50.7 0.6 %copy.8 = f32[16,256]{1,0:T(8,128)} copy(f32[16,256]{1,0:T(8,128)S(1)} %shard_map.64) | data formatting | bytes 32768
Async XLA Ops:
  0.0 1.6 %copy-start = (f32[128,4096]{1,0:T(8,128)S(1)}, f32[128,4096]{1,0:T(8,128)}, u32[]{:S(2)}) copy-start(f32[128,4096]{1,0:T(8,128)} %queries_ref.1) | copy-start | bytes 6291460
  1.6 0.9 %copy-start.1 = (bf16[1024,64]{0,1:T(8,128)(2,1)S(1)}, bf16[1024,64]{0,1:T(8,128)(2,1)}, u32[]{:S(2)}) copy-start(bf16[1024,64]{0,1:T(8,128)(2,1)} %param.8) | copy-start | bytes 393220
  2.5 0.9 %copy-start.2 = (bf16[1024,64]{0,1:T(8,128)(2,1)S(1)}, bf16[1024,64]{0,1:T(8,128)(2,1)}, u32[]{:S(2)}) copy-start(bf16[1024,64]{0,1:T(8,128)(2,1)} %param.9) | copy-start | bytes 393220
  3.4 0.7 %copy-start.3 = (s32[16]{0:T(128)S(1)}, s32[16]{0:T(128)}, u32[]{:S(2)}) copy-start(s32[16]{0:T(128)} %param.10) | copy-start | bytes 196
